TPU v7x, 128 devices: a whole 4x4x4 slice. The times are simulated.
128 devices in a mesh: src: 8 (over x, y_lo), tgt: 16 (over y_hi, z, core).
Axes of the slice: x: 4, y: 4 (y_hi: 2, y_lo: 2; y = y_hi * 2 + y_lo), z: 4, core: 2. Of those that a mesh axis runs over, the one named last changes fastest.
Arguments:
- source_weights: bfloat16 [16, 16, 1024, 128], P('src', 'tgt'), may hold values from -6 to 6
- wave_speed: float32 [2, 3], replicated, may hold values from 0.25 to 1
- offsets: float32 [32, 4], replicated, may hold values from 1 to 2
Outputs:
- target_weights: float32 [16, 16, 1024, 128], P(None, None, ('src', 'tgt'))
All inputs are finite; a program needn't handle non-finite values.
Results may differ from a plain program's by a relative error of at most 0.0003.
Values sent between devices are 32-bit elements; how exact they have to be, the bound alone decides.
A program may use at most 64 MiB of HBM per device.

v0:
```python
import functools
import math

import jax
import jax.numpy as jnp
import numpy as np
from jax import lax
from jax.experimental import pallas as pl
from jax.experimental.pallas import tpu as pltpu
from jax.sharding import PartitionSpec as P

POINTS = 8
PHASE_SCALE = 4096.0
F32 = jnp.float32
BF16 = jnp.bfloat16


def nodes():
    return 0.5 - 0.5 * np.cos((2.0 * np.arange(8) + 1.0) * (math.pi / 16.0))


def basis(axis):
    z = nodes()
    out = np.zeros((2, 2, 8, 8, 2, 8, 8))
    for s in range(2):
        for p in range(8):
            u = (s + z[p]) / 2.0
            for t in range(8):
                value = 1.0
                for a in range(8):
                    if a != t:
                        value *= (u - z[a]) / (z[t] - z[a])
                for h in range(2):
                    for q in range(8):
                        if axis == 0:
                            out[s, h, p, q, h, t, q] = value
                        else:
                            out[s, h, q, p, h, q, t] = value
    return out.reshape(256, 128)


def basis_split():
    both = []
    for axis in range(2):
        full = basis(axis).astype(np.float32)
        high = full.astype(jnp.bfloat16)
        low = (full - high.astype(np.float32)).astype(jnp.bfloat16)
        both.append(np.concatenate([high, low], axis=1))
    return np.stack(both)


def lane_tables():
    z = nodes().astype(np.float32)
    lane = np.arange(128)
    s, p1, p2 = lane // 64, lane // 8 % 8, lane % 8
    out = np.zeros((8, 4, 128), np.float32)
    for level in range(8):
        k1, k2 = level // 2 + 1, (level + 1) // 2
        w1, w2 = np.float32(2.0 ** (k1 - 10)), np.float32(2.0 ** (k2 - 10))
        if level % 2 == 0:
            out[level, 0] = w1 / 2 * (s.astype(np.float32) + z[p1])
            out[level, 1] = w2 * z[p2]
        else:
            out[level, 0] = w1 * z[p1]
            out[level, 1] = w2 / 2 * (s.astype(np.float32) + z[p2])
        out[level, 2] = w1 * z[p1]
        out[level, 3] = w2 * z[p2]
    return out


def sine_cosine(angle):
    turns = jnp.round(angle * (1.0 / math.pi))
    rest = angle - turns * 3.140625
    rest = rest - turns * 9.67502593994140625e-4
    rest = rest - turns * 1.509957990978376432e-7
    odd = (turns.astype(jnp.int32) & 1) == 1
    sign = jnp.where(odd, -1.0, 1.0)
    sq = rest * rest
    sine = ((2.5997509e-6 * sq - 1.9806479e-4) * sq + 8.3330154e-3) * sq - 1.6666657e-1
    sine = sine * (sq * rest) + rest
    cosine = (2.337661e-5 * sq - 1.3865138e-3) * sq + 4.1665433e-2
    cosine = (cosine * sq - 0.5) * sq + 1.0
    return sine * sign, cosine * sign


def target_index(box, done):
    return box >> (4 - done)


def source_index(box, done):
    total = None
    for place in range(4 - done):
        bit = ((box >> place) & 1) << (3 - done - place)
        total = bit if total is None else total + bit
    return total


def place_of(box, done, target_anchor, source_anchor):
    x = target_anchor + (target_index(box, done).astype(F32) + 0.5) * (2.0 ** (-2 - done))
    source = source_index(box, done)
    if source is None:
        r = source_anchor + jnp.zeros_like(x)
    else:
        r = source_anchor + source.astype(F32) * (2.0 ** (done - 10))
    return x, r


def angle_of(speed, x1, r1, x2, r2, d1, d2):
    s1 = speed[0] + speed[1] * x1 + speed[2] * x2
    s2 = speed[3] + speed[4] * x1 + speed[5] * x2
    a1, a2 = s1 * s1, s2 * s2
    k1, k2 = r1 + d1, r2 + d2
    over = a1 * (d1 * (k1 + r1)) + a2 * (d2 * (k2 + r2))
    under = jnp.sqrt(a1 * (k1 * k1) + a2 * (k2 * k2)) + jnp.sqrt(a1 * (r1 * r1) + a2 * (r2 * r2))
    return PHASE_SCALE * ((x1 * d1 + x2 * d2) + over / under)


def merge_place(level):
    return 3 - level // 2


def make_tables(level, speed, anchor, lanes_ref, cos_ref, sin_ref):
    lane = lax.broadcasted_iota(jnp.int32, (8, 128), 1)
    row = lax.broadcasted_iota(jnp.int32, (8, 128), 0)
    upper = lane >= 64
    side = jnp.where(upper, 1, 0)
    place = merge_place(level)

    def done(which):
        return which // 2 + 1, (which + 1) // 2

    def step(j, carry):
        jv = jnp.zeros((8, 128), jnp.int32) + j
        for half in range(2):
            iv = row + 8 * half
            angle = None
            if level < 8:
                k1, k2 = done(level)
                x1, r1 = place_of(iv, k1, anchor[0], anchor[2])
                x2, r2 = place_of(jv, k2, anchor[1], anchor[3])
                d1, d2 = lanes_ref[level, 0:1, :], lanes_ref[level, 1:2, :]
                angle = angle_of(speed, x1, r1, x2, r2, d1, d2)
            if level > 0:
                k1, k2 = done(level - 1)
                io, jo = iv, jv
                if level < 8 and level % 2 == 0:
                    io = (iv & ~(1 << place)) | (side << place)
                elif level < 8:
                    jo = (jv & ~(1 << place)) | (side << place)
                x1, r1 = place_of(io, k1, anchor[0], anchor[2])
                x2, r2 = place_of(jo, k2, anchor[1], anchor[3])
                d1, d2 = lanes_ref[level - 1, 2:3, :], lanes_ref[level - 1, 3:4, :]
                out = angle_of(speed, x1, r1, x2, r2, d1, d2)
                angle = -out if angle is None else angle - out
            sine, cosine = sine_cosine(angle)
            rows = pl.ds(pl.multiple_of(j * 16 + 8 * half, 8), 8)
            if level < 8:
                sine_r = pltpu.roll(sine, 64, 1)
                cosine_r = pltpu.roll(cosine, 64, 1)
                cos_ref[level, 0, rows, :] = jnp.where(upper, cosine_r, cosine)
                cos_ref[level, 1, rows, :] = jnp.where(upper, cosine, cosine_r)
                sin_ref[level, 0, rows, :] = jnp.where(upper, sine_r, -sine)
                sin_ref[level, 1, rows, :] = jnp.where(upper, sine, -sine_r)
            else:
                cos_ref[level, 0, rows, :] = cosine
                sin_ref[level, 0, rows, :] = jnp.where(upper, sine, -sine)
        return carry

    lax.fori_loop(0, 16, step, 0)


def spread(table, level, side, rows):
    return jnp.concatenate(
        [jnp.broadcast_to(table[level, side, pl.ds(r, 1), :], (8, 128)) for r in rows], axis=0
    )


def halves(value):
    high = value.astype(BF16)
    low = (value - high.astype(F32)).astype(BF16)
    return high, low


def merge(level, lower, upper, kids, cos_ref, sin_ref, weights):
    lower_r = pltpu.roll(lower, 64, 1)
    upper_r = pltpu.roll(upper, 64, 1)
    blocks = []
    for rows in kids:
        low = lower * spread(cos_ref, level, 0, rows) + lower_r * spread(sin_ref, level, 0, rows)
        up = upper * spread(cos_ref, level, 1, rows) + upper_r * spread(sin_ref, level, 1, rows)
        blocks.append((halves(low), halves(up)))
    high = jnp.concatenate([jnp.concatenate([b[0][0], b[1][0]], axis=1) for b in blocks], axis=0)
    rest = jnp.concatenate([jnp.concatenate([b[0][1], b[1][1]], axis=1) for b in blocks], axis=0)
    both = jnp.dot(high, weights, preferred_element_type=F32)
    both = both + jnp.dot(rest, weights, preferred_element_type=F32)
    return both[:, :128] + both[:, 128:]


def levels_kernel(speed_ref, offset_ref, lanes_ref, basis_ref, in_ref, out_ref, data, cos_ref, sin_ref):
    me = lax.axis_index("src") * lax.axis_size("tgt") + lax.axis_index("tgt")
    group = me * 8 // 32
    anchor = [offset_ref[group, c] for c in range(4)]
    speed = [speed_ref[a, b] for a in range(2) for b in range(3)]
    for level in range(9):
        make_tables(level, speed, anchor, lanes_ref, cos_ref, sin_ref)

    def load(j, carry):
        for s in range(8):
            data[j, 2 * s : 2 * s + 2] = in_ref[s, j]
        return carry

    lax.fori_loop(0, 16, load, 0)

    for level in range(8):
        place = merge_place(level)
        weights = basis_ref[level % 2]
        if level % 2 == 0:

            def step(jj, carry, level=level, place=place, weights=weights):
                low_i = [i for i in range(16) if not i >> place & 1]
                js = [2 * jj, 2 * jj + 1]
                lower = jnp.concatenate([data[j, i] for j in js for i in low_i], axis=0)
                upper = jnp.concatenate([data[j, i + (1 << place)] for j in js for i in low_i], axis=0)
                kids = [[j * 16 + i + (c << place) for j in js for i in low_i] for c in range(2)]
                result = merge(level, lower, upper, kids, cos_ref, sin_ref, weights)
                at = 0
                for c in range(2):
                    for j in js:
                        for i in low_i:
                            data[j, i + (c << place)] = result[at : at + 8]
                            at += 8
                return carry

            lax.fori_loop(0, 8, step, 0)
        else:

            def step(jj, carry, level=level, place=place, weights=weights):
                j0 = (jj >> place) * (2 << place) + (jj & ((1 << place) - 1))
                j1 = j0 + (1 << place)
                lower = jnp.concatenate([data[j0, i] for i in range(16)], axis=0)
                upper = jnp.concatenate([data[j1, i] for i in range(16)], axis=0)
                kids = [[j * 16 + i for i in range(16)] for j in (j0, j1)]
                result = merge(level, lower, upper, kids, cos_ref, sin_ref, weights)
                at = 0
                for j in (j0, j1):
                    for i in range(16):
                        block = result[at : at + 8]
                        at += 8
                        if level < 7:
                            data[j, i] = block
                        else:
                            row = [j * 16 + i]
                            out_ref[i, j] = block * spread(cos_ref, 8, 0, row) + pltpu.roll(
                                block, 64, 1
                            ) * spread(sin_ref, 8, 0, row)
                return carry

            lax.fori_loop(0, 8, step, 0)


def on_device(source_weights, wave_speed, offsets):
    widened = source_weights.astype(F32)
    received = lax.all_to_all(widened, ("src", "tgt"), split_axis=2, concat_axis=0, tiled=True)
    received = received.reshape(8, 16, 2, 8, 128)
    vmem = pl.BlockSpec(memory_space=pltpu.VMEM)
    smem = pl.BlockSpec(memory_space=pltpu.SMEM)
    return pl.pallas_call(
        levels_kernel,
        out_shape=jax.ShapeDtypeStruct((16, 16, 8, 128), F32),
        in_specs=[smem, smem, vmem, vmem, vmem],
        out_specs=vmem,
        scratch_shapes=[
            pltpu.VMEM((16, 16, 8, 128), F32),
            pltpu.VMEM((9, 2, 256, 128), F32),
            pltpu.VMEM((9, 2, 256, 128), F32),
        ],
        compiler_params=pltpu.CompilerParams(vmem_limit_bytes=48 << 20),
    )(wave_speed, offsets, jnp.asarray(lane_tables()), jnp.asarray(basis_split()), received)


def solution(mesh):
    in_specs = (P("src", "tgt", None, None), P(), P())
    out_specs = P(None, None, ("src", "tgt"), None)
    return jax.shard_map(
        on_device, mesh=mesh, in_specs=in_specs, out_specs=out_specs, check_vma=False
    )
```

profile of v0, /device:TPU:1, one launch (start us, length us, event | category | flops | bytes accessed | tf_op | source)
XLA Modules:
  0.0 72.3 jit_solution(2389580256467342786)
XLA Ops:
  0.0 2.5 %copy.14 = f32[2,1,1024,128]{3,0,1,2:T(2,128)} copy(bf16[2,1,1024,128]{3,2,1,0:T(8,128)(2,1)} %param.5) | data formatting | bytes 1572864 | tf_op jit(solution)/shard_map/convert_element_type | solution.py:262
  2.6 0.0 copy-start.3
  2.6 11.5 %all-to-all-start = ((f32[2,1,1024,128]{3,0,1,2:T(2,128)}), f32[2,1,1024,128]{3,0,1,2:T(2,128)S(1)}, u32[]{:S(2)}, u32[]{:S(2)}) async-start(f32[2,1,1024,128]{3,0,1,2:T(2,128)} %copy.14), calls=%async_computation | async-start | bytes 2097152 | tf_op jit(solution)/shard_map/all_to_all | solution.py:263
  14.1 0.0 copy-done.3
  14.1 0.1 copy.16.offset_ref
  14.2 18.8 %all-to-all-done = f32[2,1,1024,128]{3,0,1,2:T(2,128)S(1)} async-done(((f32[2,1,1024,128]{3,0,1,2:T(2,128)}), f32[2,1,1024,128]{3,0,1,2:T(2,128)S(1)}, u32[]{:S(2)}, u32[]{:S(2)}) %all-to-all-start) | async-done | bytes 1048608 | tf_op jit(solution)/shard_map/all_to_all | solution.py:263
  33.0 0.0 copy-start
  33.0 0.0 copy-start.1
  33.0 0.1 copy.15
  33.1 0.0 copy-start.2
  33.1 0.9 %copy-done = bf16[2,256,256]{2,1,0:T(8,128)(2,1)S(1)} copy-done((bf16[2,256,256]{2,1,0:T(8,128)(2,1)S(1)}, bf16[2,256,256]{2,1,0:T(8,128)(2,1)}, u32[]{:S(2)}) %copy-start) | copy-done | bytes 262168
  33.9 0.0 copy-done.1
  33.9 0.0 copy-done.2
  33.9 38.3 %shard_map.55 = f32[16,16,8,128]{3,2,1,0:T(8,128)} custom-call(f32[2,3]{1,0:T(2,128)S(1)} %copy-done.2, f32[32,4]{1,0:T(8,128)S(1)} %copy.16.offset_ref, f32[8,4,128]{2,1,0:T(4,128)S(1)} %copy-done.1, bf16[2,256,256]{2,1,0:T(8,128)(2,1)S(1)} %copy-done, f32[8,16,2,8,128]{4,3,2,1,0:T(8,128)S(1)} %bitcast.4), custom_call_target="tpu_custom_call" | custom-call | tf_op jit(solution)/shard_map/pallas_call | solution.py:267
Async XLA Ops:
  2.6 11.5 %copy-start.3 = (f32[32,4]{0,1:T(4,128)S(1)}, f32[32,4]{0,1:T(4,128)}, u32[]{:S(2)}) copy-start(f32[32,4]{0,1:T(4,128)} %param.7) | copy-start | bytes 1540
  2.6 30.4 %all-to-all-start = ((f32[2,1,1024,128]{3,0,1,2:T(2,128)}), f32[2,1,1024,128]{3,0,1,2:T(2,128)S(1)}, u32[]{:S(2)}, u32[]{:S(2)}) async-start(f32[2,1,1024,128]{3,0,1,2:T(2,128)} %copy.14), calls=%async_computation | async-start | bytes 2097152 | tf_op jit(solution)/shard_map/all_to_all | solution.py:263
  33.0 1.0 %copy-start = (bf16[2,256,256]{2,1,0:T(8,128)(2,1)S(1)}, bf16[2,256,256]{2,1,0:T(8,128)(2,1)}, u32[]{:S(2)}) copy-start(bf16[2,256,256]{2,1,0:T(8,128)(2,1)} %constant.5.clone.basis_ref) | copy-start | bytes 786436
  33.0 1.0 %copy-start.1 = (f32[8,4,128]{2,1,0:T(4,128)S(1)}, f32[8,4,128]{2,1,0:T(4,128)}, u32[]{:S(2)}) copy-start(f32[8,4,128]{2,1,0:T(4,128)} %constant.4.clone.lanes_ref) | copy-start | bytes 49156
  33.1 0.9 %copy-start.2 = (f32[2,3]{1,0:T(2,128)S(1)}, f32[2,3]{1,0:T(2,128)}, u32[]{:S(2)}) copy-start(f32[2,3]{1,0:T(2,128)} %speed_ref.1) | copy-start | bytes 76
where the time goes:
time: 72.5 us; the launch traced here: 72.3 us
  Pallas kernels  38.3 us (53%)
  waiting for transfers between devices  18.8 us (26%)
  starting transfers between devices  11.5 us (16%)
  local copies, waits for them, and re-layouts  3.58 us (5%)
    pallas_call x1, Pallas kernels, on_device(): pl.pallas_call(levels_kernel, out_shape=jax.ShapeDtypeStruct((16, 16, 8,...  38.3 us
    all_to_all x1, waiting for transfers between devices, on_device(): lax.all_to_all(widened, ('src', 'tgt'), split_axis=2, concat_axis=0, tile...  18.8 us
    all_to_all x1, starting transfers between devices, on_device(): lax.all_to_all(widened, ('src', 'tgt'), split_axis=2, concat_axis=0, tile...  11.5 us
    convert_element_type x1, local copies, waits for them, and re-layouts, on_device(): widened = source_weights.astype(F32)  2.55 us
  transfers between devices with their start and end apart: 1, of which 1 were waited for; matrix products, arithmetic and copies ran while one was open for 0% of the time, Pallas kernels for 0%

commit v1 on v0

v1 whole, which is shorter than its diff:
```python
import functools
import math

import jax
import jax.numpy as jnp
import numpy as np
from jax import lax
from jax.experimental import pallas as pl
from jax.experimental.pallas import tpu as pltpu
from jax.sharding import PartitionSpec as P

POINTS = 8
HALF_SCALE = 2048.0
MESH = pl.DeviceIdType.MESH
F32 = jnp.float32
BF16 = jnp.bfloat16


def nodes():
    return 0.5 - 0.5 * np.cos((2.0 * np.arange(8) + 1.0) * (math.pi / 16.0))


def basis(axis):
    z = nodes()
    out = np.zeros((2, 2, 8, 8, 2, 8, 8))
    for s in range(2):
        for p in range(8):
            u = (s + z[p]) / 2.0
            for t in range(8):
                value = 1.0
                for a in range(8):
                    if a != t:
                        value *= (u - z[a]) / (z[t] - z[a])
                for h in range(2):
                    for q in range(8):
                        if axis == 0:
                            out[s, h, p, q, h, t, q] = value
                        else:
                            out[s, h, q, p, h, q, t] = value
    return out.reshape(256, 128)


def basis_split():
    both = []
    for axis in range(2):
        full = basis(axis).astype(np.float32)
        high = full.astype(jnp.bfloat16)
        low = (full - high.astype(np.float32)).astype(jnp.bfloat16)
        both.append(np.concatenate([high, high, low], axis=0))
    return np.stack(both)


def lane_tables():
    z = nodes().astype(np.float32)
    lane = np.arange(128)
    s, p1, p2 = lane // 64, lane // 8 % 8, lane % 8
    out = np.zeros((8, 4, 128), np.float32)
    for level in range(8):
        k1, k2 = level // 2 + 1, (level + 1) // 2
        w1, w2 = np.float32(2.0 ** (k1 - 10)), np.float32(2.0 ** (k2 - 10))
        if level % 2 == 0:
            out[level, 0] = w1 / 2 * (s.astype(np.float32) + z[p1])
            out[level, 1] = w2 * z[p2]
        else:
            out[level, 0] = w1 * z[p1]
            out[level, 1] = w2 / 2 * (s.astype(np.float32) + z[p2])
        out[level, 2] = w1 * z[p1]
        out[level, 3] = w2 * z[p2]
    return out


def sine_cosine(half):
    turns = half * (1.0 / math.pi) + 12582912.0
    turns = turns - 12582912.0
    rest = half - turns * 3.140625
    rest = rest - turns * 9.67653589793e-4
    sq = rest * rest
    sine = ((5.1995018e-6 * sq - 3.9612958e-4) * sq + 1.66660308e-2) * sq - 3.3333314e-1
    sine = (sine * sq + 2.0) * rest
    cosine = (2.337661e-5 * sq - 1.3865138e-3) * sq + 4.1665433e-2
    cosine = (cosine * sq - 0.5) * sq + 1.0
    return sine * cosine, 1.0 - 0.5 * (sine * sine)


def source_index(box, done):
    total = box * 0
    for place in range(4 - done):
        total = total + (((box >> place) & 1) << (3 - done - place))
    return total


def part_of(box, done, target_anchor, source_anchor, slopes, shifts, delta):
    x = target_anchor + ((box >> (4 - done)).astype(F32) + 0.5) * (2.0 ** (-2 - done))
    r = source_anchor + source_index(box, done).astype(F32) * (2.0 ** (done - 10))
    first, second = slopes[0] * x, slopes[1] * x
    if shifts is not None:
        first, second = shifts[0] + first, shifts[1] + second
    k = r + delta
    scaled = delta * HALF_SCALE
    return first, second, scaled * (k + r), k * k, r * r, x * scaled


def half_angle(one, two):
    s1, s2 = one[0] + two[0], one[1] + two[1]
    a1, a2 = s1 * s1, s2 * s2
    over = a1 * one[2] + a2 * two[2]
    there = a1 * one[3] + a2 * two[3]
    here = a1 * one[4] + a2 * two[4]
    under = there * lax.rsqrt(there) + here * lax.rsqrt(here)
    return (one[5] + two[5]) + over / under


def merge_place(level):
    return 3 - level // 2


def make_tables(level, speed, anchor, lanes_ref, cos_ref, sin_ref):
    lane = lax.broadcasted_iota(jnp.int32, (8, 128), 1)
    row = lax.broadcasted_iota(jnp.int32, (8, 128), 0)
    upper = lane >= 64
    side = jnp.where(upper, 1, 0)
    place = merge_place(level)
    low = (1 << place) - 1 if level < 8 else 0

    def first(box, at, which):
        return part_of(
            box, at // 2 + 1, anchor[0], anchor[2], (speed[1], speed[4]), (speed[0], speed[3]),
            lanes_ref[at, which : which + 1, :],
        )

    def second(box, at, which):
        return part_of(
            box, (at + 1) // 2, anchor[1], anchor[3], (speed[2], speed[5]), None,
            lanes_ref[at, which : which + 1, :],
        )

    def store(angle, at):
        sine, cosine = sine_cosine(angle)
        rows = pl.ds(pl.multiple_of(at, 8), 8)
        if level < 8:
            sine_r = pltpu.roll(sine, 64, 1)
            cosine_r = pltpu.roll(cosine, 64, 1)
            cos_ref[level, 0, rows, :] = jnp.where(upper, cosine_r, cosine)
            cos_ref[level, 1, rows, :] = jnp.where(upper, cosine, cosine_r)
            sin_ref[level, 0, rows, :] = jnp.where(upper, sine_r, -sine)
            sin_ref[level, 1, rows, :] = jnp.where(upper, sine, -sine_r)
        else:
            cos_ref[level, 0, rows, :] = cosine
            sin_ref[level, 0, rows, :] = jnp.where(upper, sine, -sine)

    if level == 8:
        ones = [first(row + 8 * half, 7, 2) for half in range(2)]

        def step(jj, carry):
            for j in (2 * jj, 2 * jj + 1):
                two = second(j, 7, 3)
                for half in range(2):
                    store(-half_angle(ones[half], two), j * 16 + 8 * half)
            return carry

    elif level % 2 == 0:
        pair = ((row & ~low) << 1) | (row & low)
        ones = [first(pair | (c << place), level, 0) for c in range(2)]
        if level > 0:
            outs = first(pair | (side << place), level - 1, 2)

        def step(jj, carry):
            for j in (2 * jj, 2 * jj + 1):
                two = second(j, level, 1)
                if level > 0:
                    out = half_angle(outs, second(j, level - 1, 3))
                for c in range(2):
                    angle = half_angle(ones[c], two)
                    if level > 0:
                        angle = angle - out
                    store(angle, j * 16 + 8 * c)
            return carry

    else:
        ones = [first(row + 8 * half, level, 0) for half in range(2)]
        outs = [first(row + 8 * half, level - 1, 2) for half in range(2)]

        def step(jj, carry):
            j0 = ((jj >> place) << (place + 1)) | (jj & low)
            two_out = second(j0 + (side << place), level - 1, 3)
            out = [half_angle(outs[half], two_out) for half in range(2)]
            for c in range(2):
                j = j0 + (c << place)
                two = second(j, level, 1)
                for half in range(2):
                    store(half_angle(ones[half], two) - out[half], j * 16 + 8 * half)
            return carry

    lax.fori_loop(0, 8, step, 0)


def spread(table, level, side, rows):
    return jnp.concatenate(
        [jnp.broadcast_to(table[level, side, pl.ds(r, 1), :], (8, 128)) for r in rows], axis=0
    )


def halves(value):
    high = value.astype(BF16)
    low = (value - high.astype(F32)).astype(BF16)
    return high, low


def merge(level, lower, upper, kids, cos_ref, sin_ref, weights):
    lower_r = pltpu.roll(lower, 64, 1)
    upper_r = pltpu.roll(upper, 64, 1)
    blocks = []
    for rows in kids:
        low = lower * spread(cos_ref, level, 0, rows) + lower_r * spread(sin_ref, level, 0, rows)
        up = upper * spread(cos_ref, level, 1, rows) + upper_r * spread(sin_ref, level, 1, rows)
        (low_h, low_r), (up_h, up_r) = halves(low), halves(up)
        blocks.append(jnp.concatenate([low_h, up_h, low_r, up_r, low_h, up_h], axis=1))
    return jnp.dot(jnp.concatenate(blocks, axis=0), weights, preferred_element_type=F32)


def merge_first(level, js, data, cos_ref, sin_ref, basis_ref):
    place = merge_place(level)
    low_i = [i for i in range(16) if not i >> place & 1]
    high_i = [i + (1 << place) for i in low_i]
    lower = jnp.concatenate([data[j, i] for j in js for i in low_i], axis=0)
    upper = jnp.concatenate([data[j, i] for j in js for i in high_i], axis=0)
    kids = [[j * 16 + 8 * c + p for j in js for p in range(8)] for c in range(2)]
    result = merge(level, lower, upper, kids, cos_ref, sin_ref, basis_ref[0])
    at = 0
    for into in (low_i, high_i):
        for j in js:
            for i in into:
                data[j, i] = result[at : at + 8]
                at += 8


def merge_second(level, pairs, data, cos_ref, sin_ref, basis_ref, out_ref=None):
    lower = jnp.concatenate([data[j0, i] for j0, _ in pairs for i in range(16)], axis=0)
    upper = jnp.concatenate([data[j1, i] for _, j1 in pairs for i in range(16)], axis=0)
    kids = [[pair[c] * 16 + i for pair in pairs for i in range(16)] for c in range(2)]
    result = merge(level, lower, upper, kids, cos_ref, sin_ref, basis_ref[1])
    at = 0
    for c in range(2):
        for pair in pairs:
            for i in range(16):
                block = result[at : at + 8]
                at += 8
                if out_ref is None:
                    data[pair[c], i] = block
                else:
                    row = [pair[c] * 16 + i]
                    out_ref[i, pair[c]] = block * spread(cos_ref, 8, 0, row) + pltpu.roll(
                        block, 64, 1
                    ) * spread(sin_ref, 8, 0, row)


def kernel(speed_ref, offset_ref, lanes_hbm, basis_hbm, in_hbm, out_ref,
           narrow, wide, data, cos_ref, sin_ref, lanes_ref, basis_ref, load_sem, send_sem, recv_sem):
    src, tgt = lax.axis_index("src"), lax.axis_index("tgt")
    me = src * 16 + tgt
    n = 128

    def peer(a, b):
        return lax.rem(src + a, 8), lax.rem(tgt + b, 16)

    barrier = pltpu.get_barrier_semaphore()
    for a in range(8):
        for b in range(16):
            if a or b:
                pl.semaphore_signal(barrier, inc=1, device_id=peer(a, b), device_id_type=MESH)
    loads = [
        pltpu.make_async_copy(in_hbm, narrow, load_sem.at[0]),
        pltpu.make_async_copy(lanes_hbm, lanes_ref, load_sem.at[1]),
        pltpu.make_async_copy(basis_hbm, basis_ref, load_sem.at[2]),
    ]
    for load in loads:
        load.start()
    loads[0].wait()

    def widen(q, carry):
        cols = pl.ds(pl.multiple_of(q * 32, 32), 32)
        for r in range(2):
            rows = narrow[r, cols, :].astype(F32)
            for c in range(4):
                wide[q * 4 + c, r] = rows[8 * c : 8 * c + 8]
        return carry

    lax.fori_loop(0, n // 4, widen, 0)
    pl.semaphore_wait(barrier, n - 1)

    pltpu.make_async_copy(wide.at[me], data.at[tgt, src], recv_sem.at[0]).start()

    def send(a, b):
        to = peer(a, b)
        pltpu.make_async_remote_copy(
            src_ref=wide.at[to[0] * 16 + to[1]],
            dst_ref=data.at[tgt, src],
            send_sem=send_sem,
            recv_sem=recv_sem.at[b],
            device_id=to,
            device_id_type=MESH,
        ).start()

    for b in (0, 8, 4, 12, 2, 10, 6, 14, 1, 9, 5, 13, 3, 11, 7, 15):
        for a in range(8):
            if a or b:
                send(a, b)

    loads[1].wait()
    loads[2].wait()
    group = me * 8 // 32
    anchor = [offset_ref[group, c] for c in range(4)]
    speed = [speed_ref[a, b] for a in range(2) for b in range(3)]
    for level in range(9):
        make_tables(level, speed, anchor, lanes_ref, cos_ref, sin_ref)

    boxes = data.reshape(16, 16, 8, 128)
    args = (boxes, cos_ref, sin_ref, basis_ref)

    def eighth(b):
        for part in (b, b + 8):
            here = data.at[lax.rem(tgt - part + 16, 16)]
            pltpu.make_async_copy(here, here, recv_sem.at[part]).wait()
        j0 = lax.rem(tgt - b + 16, 8)
        merge_first(0, [j0, j0 + 8], *args)
        merge_second(1, [(j0, j0 + 8)], *args)
        merge_first(2, [j0, j0 + 8], *args)

    def quarter(b):
        def step(p, carry):
            eighth(b + 4 * p)
            return carry

        lax.fori_loop(0, 2, step, 0)
        j0 = lax.rem(tgt - b + 16, 4)
        merge_second(3, [(j0, j0 + 4), (j0 + 8, j0 + 12)], *args)
        merge_first(4, [j0, j0 + 4, j0 + 8, j0 + 12], *args)

    def half(b, carry):
        def step(q, carry):
            quarter(b + 2 * q)
            return carry

        lax.fori_loop(0, 2, step, 0)
        j0 = lax.rem(tgt - b + 16, 2)

        def five(k, carry):
            j = j0 + 8 * k
            merge_second(5, [(j, j + 2), (j + 4, j + 6)], *args)
            return carry

        def six(k, carry):
            j = j0 + 8 * k
            merge_first(6, [j, j + 2, j + 4, j + 6], *args)
            return carry

        lax.fori_loop(0, 2, five, 0)
        lax.fori_loop(0, 2, six, 0)
        return carry

    lax.fori_loop(0, 2, half, 0)

    def seven(k, carry):
        merge_second(7, [(4 * k, 4 * k + 1), (4 * k + 2, 4 * k + 3)], *args, out_ref=out_ref)
        return carry

    lax.fori_loop(0, 4, seven, 0)
    sent = wide.at[pl.ds(0, n - 1)]
    pltpu.make_async_copy(sent, sent, send_sem).wait()


def on_device(source_weights, wave_speed, offsets):
    vmem = pl.BlockSpec(memory_space=pltpu.VMEM)
    smem = pl.BlockSpec(memory_space=pltpu.SMEM)
    anywhere = pl.BlockSpec(memory_space=pl.ANY)
    return pl.pallas_call(
        kernel,
        out_shape=jax.ShapeDtypeStruct((16, 16, 8, 128), F32),
        in_specs=[smem, smem, anywhere, anywhere, anywhere],
        out_specs=vmem,
        scratch_shapes=[
            pltpu.VMEM((2, 1024, 128), BF16),
            pltpu.VMEM((128, 2, 8, 128), F32),
            pltpu.VMEM((16, 8, 2, 8, 128), F32),
            pltpu.VMEM((9, 2, 256, 128), F32),
            pltpu.VMEM((9, 2, 256, 128), F32),
            pltpu.VMEM((8, 4, 128), F32),
            pltpu.VMEM((2, 768, 128), BF16),
            pltpu.SemaphoreType.DMA((3,)),
            pltpu.SemaphoreType.DMA,
            pltpu.SemaphoreType.DMA((16,)),
        ],
        compiler_params=pltpu.CompilerParams(
            collective_id=0, has_side_effects=True, vmem_limit_bytes=48 << 20
        ),
    )(
        wave_speed,
        offsets,
        jnp.asarray(lane_tables()),
        jnp.asarray(basis_split()),
        source_weights.reshape(2, 1024, 128),
    )


def solution(mesh):
    in_specs = (P("src", "tgt", None, None), P(), P())
    out_specs = P(None, None, ("src", "tgt"), None)
    return jax.shard_map(
        on_device, mesh=mesh, in_specs=in_specs, out_specs=out_specs, check_vma=False
    )
```

time: 72.5 us -> 43.2 us (0.60)
  waiting for transfers between devices: 18.8 us -> 0 us
  starting transfers between devices: 11.5 us -> 0 us
  Pallas kernels: 38.3 us -> 39.1 us
    all_to_all x1 -> x0, waiting for transfers between devices: 18.8 us -> none  [on_device(): lax.all_to_all(widened, ('src', 'tgt'), split_axis=2, concat_axis=0, tile...]
    all_to_all x1 -> x0, starting transfers between devices: 11.5 us -> none  [on_device(): lax.all_to_all(widened, ('src', 'tgt'), split_axis=2, concat_axis=0, tile...]
    unnamed x9 -> x10, local copies, waits for them, and re-layouts: 0.97 us -> 3.8 us
    convert_element_type x1 -> x0, local copies, waits for them, and re-layouts: 2.55 us -> none  [on_device(): widened = source_weights.astype(F32)]
    pallas_call x1, Pallas kernels: 38.3 us -> 39.1 us  [on_device(): pl.pallas_call(kernel, out_shape=jax.ShapeDtypeStruct((16, 16, 8, 128), F...]
  transfers between devices with their start and end apart: 1 -> 0, of which waited for: 1 -> 0; matrix products, arithmetic and copies ran while one was open for 0% -> 0% of each run, Pallas kernels for 0% -> 0%
where the time goes in v1:
time: 43.2 us; the launch traced here: 42.9 us
  Pallas kernels  39.1 us (91%)
  local copies, waits for them, and re-layouts  3.8 us (9%)
    pallas_call x1, Pallas kernels, on_device(): pl.pallas_call(kernel, out_shape=jax.ShapeDtypeStruct((16, 16, 8, 128), F...  39.1 us
    unnamed x10, local copies, waits for them, and re-layouts  3.8 us

profile of v1, /device:TPU:1, one launch (start us, length us, event | category | flops | bytes accessed | tf_op | source)
XLA Modules:
  0.0 42.9 jit_solution(3768417786425686045)
XLA Ops:
  0.0 0.0 copy-start.2
  0.0 0.0 copy-start.3
  0.0 0.8 %copy.6.offset_ref = f32[32,4]{1,0:T(8,128)S(1)} copy(f32[32,4]{0,1:T(4,128)} %param.7) | data formatting | bytes 1024 | tf_op args[2]
  0.8 0.0 copy-done.2
  0.8 0.0 copy-done.3
  0.8 0.0 copy-start
  0.8 1.0 %copy-done = bf16[2,1,1024,128]{3,2,1,0:T(8,128)(2,1)S(1)} copy-done((bf16[2,1,1024,128]{3,2,1,0:T(8,128)(2,1)S(1)}, bf16[2,1,1024,128]{3,2,1,0:T(8,128)(2,1)}, u32[]{:S(2)}) %copy-start) | copy-done | bytes 524312
  1.8 0.0 copy-start.1
  1.8 1.0 %copy-done.1 = bf16[2,768,128]{2,1,0:T(8,128)(2,1)S(1)} copy-done((bf16[2,768,128]{2,1,0:T(8,128)(2,1)S(1)}, bf16[2,768,128]{2,1,0:T(8,128)(2,1)}, u32[]{:S(2)}) %copy-start.1) | copy-done | bytes 393240
  2.8 39.1 %shard_map.55 = f32[16,16,8,128]{3,2,1,0:T(8,128)S(1)} custom-call(f32[2,3]{1,0:T(2,128)S(1)} %copy-done.3, f32[32,4]{1,0:T(8,128)S(1)} %copy.6.offset_ref, f32[8,4,128]{2,1,0:T(4,128)S(1)} %copy-done.2, bf16[2,768,128]{2,1,0:T(8,128)(2,1)S(1)} %copy-done.1, bf16[2,1024,128]{2,1,0:T(8,128)(2,1)S(1)} %bitcast.1), custom_call_target="tpu_custom_call" | custom-call | tf_op jit(solution)/shard_map/pallas_call | solution.py:376
  42.0 1.0 %copy.8 = f32[16,16,8,128]{3,2,1,0:T(8,128)} copy(f32[16,16,8,128]{3,2,1,0:T(8,128)S(1)} %shard_map.55) | data formatting | bytes 2097152
Async XLA Ops:
  0.0 0.8 %copy-start.2 = (f32[8,4,128]{2,1,0:T(4,128)S(1)}, f32[8,4,128]{2,1,0:T(4,128)}, u32[]{:S(2)}) copy-start(f32[8,4,128]{2,1,0:T(4,128)} %constant.4.clone.lanes_hbm) | copy-start | bytes 49156
  0.0 0.8 %copy-start.3 = (f32[2,3]{1,0:T(2,128)S(1)}, f32[2,3]{1,0:T(2,128)}, u32[]{:S(2)}) copy-start(f32[2,3]{1,0:T(2,128)} %speed_ref.1) | copy-start | bytes 76
  0.8 1.0 %copy-start = (bf16[2,1,1024,128]{3,2,1,0:T(8,128)(2,1)S(1)}, bf16[2,1,1024,128]{3,2,1,0:T(8,128)(2,1)}, u32[]{:S(2)}) copy-start(bf16[2,1,1024,128]{3,2,1,0:T(8,128)(2,1)} %param.5) | copy-start | bytes 1572868
  1.8 1.0 %copy-start.1 = (bf16[2,768,128]{2,1,0:T(8,128)(2,1)S(1)}, bf16[2,768,128]{2,1,0:T(8,128)(2,1)}, u32[]{:S(2)}) copy-start(bf16[2,768,128]{2,1,0:T(8,128)(2,1)} %constant.5.clone.basis_hbm) | copy-start | bytes 1179652

commit v2 on v1

v2 whole, which is shorter than its diff:
```python
import functools
import math

import jax
import jax.numpy as jnp
import numpy as np
from jax import lax
from jax.experimental import pallas as pl
from jax.experimental.pallas import tpu as pltpu
from jax.sharding import PartitionSpec as P

POINTS = 8
HALF_SCALE = 2048.0
VMEM_BYTES = 48 << 20
AHEAD = 56
FIRST = 2
MESH = pl.DeviceIdType.MESH
F32 = jnp.float32
BF16 = jnp.bfloat16


def node_values():
    return [float(v) for v in 0.5 - 0.5 * np.cos((2.0 * np.arange(8) + 1.0) * (math.pi / 16.0))]


def pick(index, values):
    result = jnp.full(index.shape, values[0], F32)
    for at in range(1, len(values)):
        result = jnp.where(index == at, values[at], result)
    return result


def make_basis(axis, basis_ref):
    z = node_values()
    gaps = [math.prod(z[t] - z[a] for a in range(8) if a != t) for t in range(8)]
    col = lax.broadcasted_iota(jnp.int32, (16, 128), 1)

    def step(k, carry):
        row = lax.broadcasted_iota(jnp.int32, (16, 128), 0) + k * 16
        row_points, col_points = ((row >> 3) & 7, row & 7), ((col >> 3) & 7, col & 7)
        t = col_points[axis]
        u = ((row >> 7).astype(F32) + pick(row_points[axis], z)) * 0.5
        value = 1.0 / pick(t, gaps)
        for at in range(8):
            value = value * jnp.where(t == at, 1.0, u - z[at])
        same = (row_points[1 - axis] == col_points[1 - axis]) & (((row >> 6) & 1) == (col >> 6))
        high, low = halves(jnp.where(same, value, 0.0))
        rows = pl.ds(pl.multiple_of(k * 16, 16), 16)
        basis_ref[axis, rows, 0:128] = high
        basis_ref[axis, rows, 128:256] = low
        return carry

    lax.fori_loop(0, 16, step, 0)


def displacement(level, which):
    z = node_values()
    lane = lax.broadcasted_iota(jnp.int32, (8, 128), 1)
    dim = which % 2
    width = 2.0 ** ((level // 2 + 1, (level + 1) // 2)[dim] - 10)
    point = pick((lane & 7) if dim else ((lane >> 3) & 7), z)
    if which < 2 and level % 2 == dim:
        return (point + (lane >> 6).astype(F32)) * (width / 2)
    return point * width


def sine_cosine(half):
    turns = half * (1.0 / math.pi) + 12582912.0
    turns = turns - 12582912.0
    rest = half - turns * 3.140625
    rest = rest - turns * 9.67653589793e-4
    sq = rest * rest
    sine = ((5.1995018e-6 * sq - 3.9612958e-4) * sq + 1.66660308e-2) * sq - 3.3333314e-1
    sine = (sine * sq + 2.0) * rest
    cosine = (2.337661e-5 * sq - 1.3865138e-3) * sq + 4.1665433e-2
    cosine = (cosine * sq - 0.5) * sq + 1.0
    return sine * cosine, 1.0 - 0.5 * (sine * sine)


def source_index(box, done):
    total = box * 0
    for place in range(4 - done):
        total = total + (((box >> place) & 1) << (3 - done - place))
    return total


def part_of(box, done, target_anchor, source_anchor, slopes, shifts, delta):
    x = target_anchor + ((box >> (4 - done)).astype(F32) + 0.5) * (2.0 ** (-2 - done))
    r = source_anchor + source_index(box, done).astype(F32) * (2.0 ** (done - 10))
    first, second = slopes[0] * x, slopes[1] * x
    if shifts is not None:
        first, second = shifts[0] + first, shifts[1] + second
    k = r + delta
    scaled = delta * HALF_SCALE
    return first, second, scaled * (k + r), k * k, r * r, x * scaled


def half_angle(one, two):
    s1, s2 = one[0] + two[0], one[1] + two[1]
    a1, a2 = s1 * s1, s2 * s2
    over = a1 * one[2] + a2 * two[2]
    there = a1 * one[3] + a2 * two[3]
    here = a1 * one[4] + a2 * two[4]
    under = there * lax.rsqrt(there) + here * lax.rsqrt(here)
    return (one[5] + two[5]) + over / under


def merge_place(level):
    return 3 - level // 2


def make_tables(level, speed, anchor, cos_ref, sin_ref):
    lane = lax.broadcasted_iota(jnp.int32, (8, 128), 1)
    row = lax.broadcasted_iota(jnp.int32, (8, 128), 0)
    upper = lane >= 64
    side = jnp.where(upper, 1, 0)
    place = merge_place(level)
    low = (1 << place) - 1 if level < 8 else 0

    def first(box, at, which):
        return part_of(
            box, at // 2 + 1, anchor[0], anchor[2], (speed[1], speed[4]), (speed[0], speed[3]),
            displacement(at, which),
        )

    def second(box, at, which):
        return part_of(
            box, (at + 1) // 2, anchor[1], anchor[3], (speed[2], speed[5]), None,
            displacement(at, which),
        )

    def store(angle, at):
        sine, cosine = sine_cosine(angle)
        rows = pl.ds(pl.multiple_of(at, 8), 8)
        cos_ref[level, 0, rows, :] = cosine
        sin_ref[level, 0, rows, :] = sine if level < 8 else jnp.where(upper, sine, -sine)

    if level == 8:
        ones = [first(row + 8 * half, 7, 2) for half in range(2)]

        def step(jj, carry):
            for j in (2 * jj, 2 * jj + 1):
                two = second(j, 7, 3)
                for half in range(2):
                    store(-half_angle(ones[half], two), j * 16 + 8 * half)
            return carry

    elif level % 2 == 0:
        pair = ((row & ~low) << 1) | (row & low)
        ones = [first(pair | (c << place), level, 0) for c in range(2)]
        if level > 0:
            outs = first(pair | (side << place), level - 1, 2)

        def step(jj, carry):
            for j in (2 * jj, 2 * jj + 1):
                two = second(j, level, 1)
                if level > 0:
                    out = half_angle(outs, second(j, level - 1, 3))
                for c in range(2):
                    angle = half_angle(ones[c], two)
                    if level > 0:
                        angle = angle - out
                    store(angle, j * 16 + 8 * c)
            return carry

    else:
        ones = [first(row + 8 * half, level, 0) for half in range(2)]
        outs = [first(row + 8 * half, level - 1, 2) for half in range(2)]

        def step(jj, carry):
            j0 = ((jj >> place) << (place + 1)) | (jj & low)
            two_out = second(j0 + (side << place), level - 1, 3)
            out = [half_angle(outs[half], two_out) for half in range(2)]
            for c in range(2):
                j = j0 + (c << place)
                two = second(j, level, 1)
                for half in range(2):
                    store(half_angle(ones[half], two) - out[half], j * 16 + 8 * half)
            return carry

    lax.fori_loop(0, 8, step, 0)
    if level == 8:
        return

    def widen(k, carry):
        rows = [pl.ds(pl.multiple_of(k * 64 + 8 * q, 8), 8) for q in range(8)]
        sines = [sin_ref[level, 0, r, :] for r in rows]
        cosines = [cos_ref[level, 0, r, :] for r in rows]
        sines_r = [pltpu.roll(v, 64, 1) for v in sines]
        cosines_r = [pltpu.roll(v, 64, 1) for v in cosines]
        for r, sine, cosine, sine_r, cosine_r in zip(rows, sines, cosines, sines_r, cosines_r):
            cos_ref[level, 0, r, :] = jnp.where(upper, cosine_r, cosine)
            cos_ref[level, 1, r, :] = jnp.where(upper, cosine, cosine_r)
            sin_ref[level, 0, r, :] = jnp.where(upper, sine_r, -sine)
            sin_ref[level, 1, r, :] = jnp.where(upper, sine, -sine_r)
        return carry

    lax.fori_loop(0, 4, widen, 0)


def spread(table, level, side, rows):
    return jnp.concatenate(
        [jnp.broadcast_to(table[level, side, pl.ds(r, 1), :], (8, 128)) for r in rows], axis=0
    )


def halves(value):
    high = value.astype(BF16)
    low = (value - high.astype(F32)).astype(BF16)
    return high, low


def merge(level, tiles, js, cos_ref, sin_ref, basis_ref):
    place = merge_place(level)
    count = len(js)
    low = 1 << place
    if level % 2 == 0:
        starts = [i for i in range(16) if not i & low]
        pairs = [((k, i), (k, i + low)) for k in range(count) for i in starts]
        rows = [[js[k] * 16 + 8 * c + p for k in range(count) for p in range(8)] for c in range(2)]
    else:
        apart = low * count // 16
        firsts = [k for k in range(count) if not k & apart]
        pairs = [((k, i), (k + apart, i)) for k in firsts for i in range(16)]
        rows = [[js[k + c * apart] * 16 + i for k in firsts for i in range(16)] for c in range(2)]
    lower = jnp.concatenate([tiles[p] for p, _ in pairs], axis=0)
    upper = jnp.concatenate([tiles[q] for _, q in pairs], axis=0)
    lower_r = pltpu.roll(lower, 64, 1)
    upper_r = pltpu.roll(upper, 64, 1)
    high, rest = [], []
    for kid in rows:
        down = lower * spread(cos_ref, level, 0, kid) + lower_r * spread(sin_ref, level, 0, kid)
        up = upper * spread(cos_ref, level, 1, kid) + upper_r * spread(sin_ref, level, 1, kid)
        (down_h, down_r), (up_h, up_r) = halves(down), halves(up)
        high.append(jnp.concatenate([down_h, up_h], axis=1))
        rest.append(jnp.concatenate([down_r, up_r], axis=1))
    weights = basis_ref[level % 2]
    both = jnp.dot(jnp.concatenate(high, axis=0), weights, preferred_element_type=F32)
    both = both + jnp.dot(jnp.concatenate(rest, axis=0), weights, preferred_element_type=F32)
    result = both[:, :128] + both[:, 128:]
    after = [p for p, _ in pairs] + [q for _, q in pairs]
    return {at: result[8 * n : 8 * n + 8] for n, at in enumerate(after)}


def kernel(speed_hbm, offset_hbm, in_hbm, out_ref, speed_ref, offset_ref,
           narrow, wide, data, cos_ref, sin_ref, basis_ref, load_sem, send_sem, recv_sem):
    src, tgt = lax.axis_index("src"), lax.axis_index("tgt")
    me = src * 16 + tgt
    n = 128

    def peer(a, b):
        return lax.rem(src + a, 8), lax.rem(tgt + b, 16)

    loads = [
        pltpu.make_async_copy(in_hbm, narrow, load_sem.at[0]),
        pltpu.make_async_copy(speed_hbm, speed_ref, load_sem.at[1]),
        pltpu.make_async_copy(offset_hbm, offset_ref, load_sem.at[2]),
    ]
    for load in loads:
        load.start()
    barrier = pltpu.get_barrier_semaphore()
    for a in range(8):
        for b in range(16):
            if a or b:
                pl.semaphore_signal(barrier, inc=1, device_id=peer(a, b), device_id_type=MESH)
    for load in loads:
        load.wait()

    def widen(q, carry):
        cols = pl.ds(pl.multiple_of(q * 32, 32), 32)
        for r in range(2):
            rows = narrow[r, cols, :].astype(F32)
            for c in range(4):
                wide[q * 4 + c, r] = rows[8 * c : 8 * c + 8]
        return carry

    lax.fori_loop(0, n // 4, widen, 0)
    entry = 4 * (src // 2) + 5 * (src % 2 + 2 * (tgt // 8)) + 8 * (tgt // 2 % 4)
    ahead = lax.div(AHEAD - entry, 6)

    group = me * 8 // 32
    anchor = [offset_ref[c, group] for c in range(4)]
    speed = [speed_ref[a, b] for a in range(2) for b in range(3)]

    def table(level, wanted):
        @pl.when(wanted)
        def _():
            make_tables(level, speed, anchor, cos_ref, sin_ref)

    for level in range(9):
        table(level, level < ahead)
    pl.semaphore_wait(barrier, n - 1)

    pltpu.make_async_copy(wide.at[me], data.at[tgt, src], recv_sem.at[0]).start()

    def send(a, b):
        to = peer(a, b)
        pltpu.make_async_remote_copy(
            src_ref=wide.at[to[0] * 16 + to[1]],
            dst_ref=data.at[tgt, src],
            send_sem=send_sem,
            recv_sem=recv_sem.at[b],
            device_id=to,
            device_id_type=MESH,
        ).start()

    def send_eighth(k):
        for b in (k, k + 8):
            for a in range(8):
                if a or b:
                    send(a, b)

    order = (0, 4, 2, 6, 1, 5, 3, 7)
    for k in order[:FIRST]:
        send_eighth(k)
    for level in range(9):
        table(level, level >= ahead)
        for k in order[FIRST + level : FIRST + level + 1]:
            send_eighth(k)
    for axis in range(2):
        make_basis(axis, basis_ref)

    boxes = data.reshape(16, 16, 8, 128)
    tables = (cos_ref, sin_ref, basis_ref)

    def quarter(q, carry):
        b = lax.rem(q, 2) * 2 + q // 2
        for part in (b, b + 8, b + 4, b + 12):
            here = data.at[lax.rem(tgt - part + 16, 16)]
            pltpu.make_async_copy(here, here, recv_sem.at[part]).wait()
        j0 = lax.rem(tgt - b + 16, 4)
        js = [j0 + 4 * k for k in range(4)]
        tiles = {(k, i): boxes[js[k], i] for k in range(4) for i in range(16)}
        for level in range(5):
            tiles = merge(level, tiles, js, *tables)
        for (k, i), value in tiles.items():
            boxes[js[k], i] = value
        return carry

    def half(b, carry):
        lax.fori_loop(2 * b, 2 * b + 2, quarter, 0)
        j0 = lax.rem(tgt - b + 16, 2)
        js = [j0 + 2 * k for k in range(8)]
        tiles = {(k, i): boxes[js[k], i] for k in range(8) for i in range(16)}
        for level in (5, 6):
            tiles = merge(level, tiles, js, *tables)
        for (k, i), value in tiles.items():
            boxes[js[k], i] = value
        return carry

    lax.fori_loop(0, 2, half, 0)
    js = list(range(16))
    tiles = {(k, i): boxes[k, i] for k in js for i in range(16)}
    tiles = merge(7, tiles, js, *tables)
    for k in js:
        block = jnp.concatenate([tiles[k, i] for i in range(16)], axis=0)
        rows = [k * 16 + i for i in range(16)]
        block = block * spread(cos_ref, 8, 0, rows) + pltpu.roll(block, 64, 1) * spread(
            sin_ref, 8, 0, rows
        )
        for i in range(16):
            out_ref[i, k] = block[8 * i : 8 * i + 8]
    sent = wide.at[pl.ds(0, n - 1)]
    pltpu.make_async_copy(sent, sent, send_sem).wait()


def on_device(source_weights, wave_speed, offsets):
    vmem = pl.BlockSpec(memory_space=pltpu.VMEM)
    anywhere = pl.BlockSpec(memory_space=pltpu.HBM)
    return pl.pallas_call(
        kernel,
        out_shape=jax.ShapeDtypeStruct((16, 16, 8, 128), F32),
        in_specs=[anywhere, anywhere, anywhere],
        out_specs=vmem,
        scratch_shapes=[
            pltpu.SMEM((2, 3), F32),
            pltpu.SMEM((4, 32), F32),
            pltpu.VMEM((2, 1024, 128), BF16),
            pltpu.VMEM((128, 2, 8, 128), F32),
            pltpu.VMEM((16, 8, 2, 8, 128), F32),
            pltpu.VMEM((9, 2, 256, 128), F32),
            pltpu.VMEM((9, 2, 256, 128), F32),
            pltpu.VMEM((2, 256, 256), BF16),
            pltpu.SemaphoreType.DMA((3,)),
            pltpu.SemaphoreType.DMA,
            pltpu.SemaphoreType.DMA((16,)),
        ],
        compiler_params=pltpu.CompilerParams(
            collective_id=0, has_side_effects=True, vmem_limit_bytes=VMEM_BYTES
        ),
    )(wave_speed, offsets.T, source_weights.reshape(2, 1024, 128))


def solution(mesh):
    in_specs = (P("src", "tgt", None, None), P(), P())
    out_specs = P(None, None, ("src", "tgt"), None)
    return jax.shard_map(
        on_device, mesh=mesh, in_specs=in_specs, out_specs=out_specs, check_vma=False
    )
```

time: 43.2 us -> 34.2 us (0.79)
  Pallas kernels: 39.1 us -> 31.3 us
  local copies, waits for them, and re-layouts: 3.8 us -> 2.71 us
    pallas_call x1, Pallas kernels: 39.1 us -> 31.3 us  [on_device(): pl.pallas_call(kernel, out_shape=jax.ShapeDtypeStruct((16, 16, 8, 128), F...]
    unnamed x10 -> x7, local copies, waits for them, and re-layouts: 3.8 us -> 2.71 us
where the time goes in v2:
time: 34.2 us; the launch traced here: 34 us
  Pallas kernels  31.3 us (92%)
  local copies, waits for them, and re-layouts  2.71 us (8%)
    pallas_call x1, Pallas kernels, on_device(): pl.pallas_call(kernel, out_shape=jax.ShapeDtypeStruct((16, 16, 8, 128), F...  31.3 us
    unnamed x7, local copies, waits for them, and re-layouts  2.71 us

profile of v2, /device:TPU:1, one launch (start us, length us, event | category | flops | bytes accessed | tf_op | source)
XLA Modules:
  0.0 34.0 jit_solution(10077498091174781762)
XLA Ops:
  0.0 0.0 copy-start.1
  0.0 0.0 copy-start.2
  0.0 0.7 %copy-done.1 = f32[32,4]{0,1:T(4,128)S(1)} copy-done((f32[32,4]{0,1:T(4,128)S(1)}, f32[32,4]{0,1:T(4,128)}, u32[]{:S(2)}) %copy-start.1) | copy-done | bytes 536
  0.7 0.0 copy-done.2
  0.7 0.0 copy-start
  0.7 1.0 %copy-done = bf16[2,1,1024,128]{3,2,1,0:T(8,128)(2,1)S(1)} copy-done((bf16[2,1,1024,128]{3,2,1,0:T(8,128)(2,1)S(1)}, bf16[2,1,1024,128]{3,2,1,0:T(8,128)(2,1)}, u32[]{:S(2)}) %copy-start) | copy-done | bytes 524312
  1.7 31.3 %shard_map.37 = f32[16,16,8,128]{3,2,1,0:T(8,128)S(1)} custom-call(f32[2,3]{1,0:T(2,128)S(1)} %copy-done.2, f32[4,32]{1,0:T(4,128)S(1)} %bitcast.3, bf16[2,1024,128]{2,1,0:T(8,128)(2,1)S(1)} %bitcast.2), custom_call_target="tpu_custom_call" | custom-call | tf_op jit(solution)/shard_map/pallas_call | solution.py:370
  33.1 1.0 %copy.5 = f32[16,16,8,128]{3,2,1,0:T(8,128)} copy(f32[16,16,8,128]{3,2,1,0:T(8,128)S(1)} %shard_map.37) | data formatting | bytes 2097152
Async XLA Ops:
  0.0 0.7 %copy-start.1 = (f32[32,4]{0,1:T(4,128)S(1)}, f32[32,4]{0,1:T(4,128)}, u32[]{:S(2)}) copy-start(f32[32,4]{0,1:T(4,128)} %param.5) | copy-start | bytes 1540
  0.0 0.7 %copy-start.2 = (f32[2,3]{1,0:T(2,128)S(1)}, f32[2,3]{1,0:T(2,128)}, u32[]{:S(2)}) copy-start(f32[2,3]{1,0:T(2,128)} %speed_hbm.1) | copy-start | bytes 76
  0.7 1.0 %copy-start = (bf16[2,1,1024,128]{3,2,1,0:T(8,128)(2,1)S(1)}, bf16[2,1,1024,128]{3,2,1,0:T(8,128)(2,1)}, u32[]{:S(2)}) copy-start(bf16[2,1,1024,128]{3,2,1,0:T(8,128)(2,1)} %param.3) | copy-start | bytes 1572868

commit v3 on v2

--- a/solution.py
+++ b/solution.py
@@ -13,7 +13,6 @@
 HALF_SCALE = 2048.0
 VMEM_BYTES = 48 << 20
 AHEAD = 56
-FIRST = 2
 MESH = pl.DeviceIdType.MESH
 F32 = jnp.float32
 BF16 = jnp.bfloat16
@@ -242,8 +241,21 @@
     return {at: result[8 * n : 8 * n + 8] for n, at in enumerate(after)}
 
 
-def kernel(speed_hbm, offset_hbm, in_hbm, out_ref, speed_ref, offset_ref,
-           narrow, wide, data, cos_ref, sin_ref, basis_ref, load_sem, send_sem, recv_sem):
+def send_order():
+    def hops(a, b):
+        steps = (a // 2, a % 2 + 2 * (b // 8), b // 2 % 4)
+        return sum(min(step, 4 - step) for step in steps)
+
+    order = []
+    for start in (0, 2, 1, 3):
+        parts = (start, start + 8, start + 4, start + 12)
+        quarter = [((3 * i + 5 * u) % 8, b) for i in range(8) for u, b in enumerate(parts)]
+        order += sorted(quarter, key=lambda to: -hops(*to))
+    return [to for to in order if to != (0, 0)]
+
+
+def kernel(speed_hbm, offset_hbm, wide, out_ref, speed_ref, offset_ref,
+           data, cos_ref, sin_ref, basis_ref, load_sem, send_sem, recv_sem):
     src, tgt = lax.axis_index("src"), lax.axis_index("tgt")
     me = src * 16 + tgt
     n = 128
@@ -252,9 +264,8 @@
         return lax.rem(src + a, 8), lax.rem(tgt + b, 16)
 
     loads = [
-        pltpu.make_async_copy(in_hbm, narrow, load_sem.at[0]),
-        pltpu.make_async_copy(speed_hbm, speed_ref, load_sem.at[1]),
-        pltpu.make_async_copy(offset_hbm, offset_ref, load_sem.at[2]),
+        pltpu.make_async_copy(speed_hbm, speed_ref, load_sem.at[0]),
+        pltpu.make_async_copy(offset_hbm, offset_ref, load_sem.at[1]),
     ]
     for load in loads:
         load.start()
@@ -266,15 +277,6 @@
     for load in loads:
         load.wait()
 
-    def widen(q, carry):
-        cols = pl.ds(pl.multiple_of(q * 32, 32), 32)
-        for r in range(2):
-            rows = narrow[r, cols, :].astype(F32)
-            for c in range(4):
-                wide[q * 4 + c, r] = rows[8 * c : 8 * c + 8]
-        return carry
-
-    lax.fori_loop(0, n // 4, widen, 0)
     entry = 4 * (src // 2) + 5 * (src % 2 + 2 * (tgt // 8)) + 8 * (tgt // 2 % 4)
     ahead = lax.div(AHEAD - entry, 6)
 
@@ -291,12 +293,15 @@
         table(level, level < ahead)
     pl.semaphore_wait(barrier, n - 1)
 
-    pltpu.make_async_copy(wide.at[me], data.at[tgt, src], recv_sem.at[0]).start()
+    def columns(owner):
+        return wide.at[:, pl.ds(pl.multiple_of(owner * 8, 8), 8), :]
+
+    pltpu.make_async_copy(columns(me), data.at[tgt, src], recv_sem.at[0]).start()
 
     def send(a, b):
         to = peer(a, b)
         pltpu.make_async_remote_copy(
-            src_ref=wide.at[to[0] * 16 + to[1]],
+            src_ref=columns(to[0] * 16 + to[1]),
             dst_ref=data.at[tgt, src],
             send_sem=send_sem,
             recv_sem=recv_sem.at[b],
@@ -304,19 +309,10 @@
             device_id_type=MESH,
         ).start()
 
-    def send_eighth(k):
-        for b in (k, k + 8):
-            for a in range(8):
-                if a or b:
-                    send(a, b)
-
-    order = (0, 4, 2, 6, 1, 5, 3, 7)
-    for k in order[:FIRST]:
-        send_eighth(k)
+    for a, b in send_order():
+        send(a, b)
     for level in range(9):
         table(level, level >= ahead)
-        for k in order[FIRST + level : FIRST + level + 1]:
-            send_eighth(k)
     for axis in range(2):
         make_basis(axis, basis_ref)
 
@@ -360,7 +356,7 @@
         )
         for i in range(16):
             out_ref[i, k] = block[8 * i : 8 * i + 8]
-    sent = wide.at[pl.ds(0, n - 1)]
+    sent = data.reshape(128, 2, 8, 128).at[pl.ds(0, n - 1)]
     pltpu.make_async_copy(sent, sent, send_sem).wait()
 
 
@@ -370,25 +366,23 @@
     return pl.pallas_call(
         kernel,
         out_shape=jax.ShapeDtypeStruct((16, 16, 8, 128), F32),
-        in_specs=[anywhere, anywhere, anywhere],
+        in_specs=[anywhere, anywhere, vmem],
         out_specs=vmem,
         scratch_shapes=[
             pltpu.SMEM((2, 3), F32),
             pltpu.SMEM((4, 32), F32),
-            pltpu.VMEM((2, 1024, 128), BF16),
-            pltpu.VMEM((128, 2, 8, 128), F32),
             pltpu.VMEM((16, 8, 2, 8, 128), F32),
             pltpu.VMEM((9, 2, 256, 128), F32),
             pltpu.VMEM((9, 2, 256, 128), F32),
             pltpu.VMEM((2, 256, 256), BF16),
-            pltpu.SemaphoreType.DMA((3,)),
+            pltpu.SemaphoreType.DMA((2,)),
             pltpu.SemaphoreType.DMA,
             pltpu.SemaphoreType.DMA((16,)),
         ],
         compiler_params=pltpu.CompilerParams(
             collective_id=0, has_side_effects=True, vmem_limit_bytes=VMEM_BYTES
         ),
-    )(wave_speed, offsets.T, source_weights.reshape(2, 1024, 128))
+    )(wave_speed, offsets.T, source_weights.astype(F32).reshape(2, 1024, 128))
 
 
 def solution(mesh):

time: 34.2 us -> 32.4 us (0.947)
  local copies, waits for them, and re-layouts: 2.71 us -> 0.98 us
  Pallas kernels: 31.3 us -> 29.8 us
  other arithmetic: 0 us -> 1.14 us
    unnamed x7 -> x5, local copies, waits for them, and re-layouts: 2.71 us -> 0.98 us
    pallas_call x1, Pallas kernels: 31.3 us -> 29.8 us  [on_device(): pl.pallas_call(kernel, out_shape=jax.ShapeDtypeStruct((16, 16, 8, 128), F...]
    reshape x0 -> x1, other arithmetic: none -> 1.14 us  [on_device(): source_weights.astype(F32).reshape(2, 1024, 128)]
where the time goes in v3:
time: 32.4 us; the launch traced here: 32 us
  Pallas kernels  29.8 us (92%)
  other arithmetic  1.14 us (4%)
  local copies, waits for them, and re-layouts  0.98 us (3%)
    pallas_call x1, Pallas kernels, on_device(): pl.pallas_call(kernel, out_shape=jax.ShapeDtypeStruct((16, 16, 8, 128), F...  29.8 us
    reshape x1, other arithmetic, on_device(): source_weights.astype(F32).reshape(2, 1024, 128)  1.14 us
    unnamed x5, local copies, waits for them, and re-layouts  0.98 us

profile of v3, /device:TPU:1, one launch (start us, length us, event | category | flops | bytes accessed | tf_op | source)
XLA Modules:
  0.0 32.0 jit_solution(16606253924356320628)
XLA Ops:
  0.0 0.0 copy-start
  0.0 0.0 copy-start.1
  0.0 1.1 %bitcast_convert_fusion.wide = f32[2,1024,128]{2,1,0:T(8,128)S(1)} fusion(bf16[2,1,1024,128]{3,2,1,0:T(8,128)(2,1)} %param.3), kind=kLoop, calls=%fused_computation | loop fusion | flops 262144 | bytes 1572864 | tf_op jit(solution)/shard_map/reshape | solution.py:385
  1.1 0.0 copy-done
  1.2 0.0 copy-done.1
  1.2 29.8 %shard_map.37 = f32[16,16,8,128]{3,2,1,0:T(8,128)S(1)} custom-call(f32[2,3]{1,0:T(2,128)S(1)} %copy-done.1, f32[4,32]{1,0:T(4,128)S(1)} %bitcast.6, f32[2,1024,128]{2,1,0:T(8,128)S(1)} %bitcast_convert_fusion.wide), custom_call_target="tpu_custom_call" | custom-call | tf_op jit(solution)/shard_map/pallas_call | solution.py:366
  31.0 1.0 %copy.6 = f32[16,16,8,128]{3,2,1,0:T(8,128)} copy(f32[16,16,8,128]{3,2,1,0:T(8,128)S(1)} %shard_map.37) | data formatting | bytes 2097152
Async XLA Ops:
  0.0 1.1 %copy-start = (f32[32,4]{0,1:T(4,128)S(1)}, f32[32,4]{0,1:T(4,128)}, u32[]{:S(2)}) copy-start(f32[32,4]{0,1:T(4,128)} %param.5) | copy-start | bytes 1540
  0.0 1.2 %copy-start.1 = (f32[2,3]{1,0:T(2,128)S(1)}, f32[2,3]{1,0:T(2,128)}, u32[]{:S(2)}) copy-start(f32[2,3]{1,0:T(2,128)} %speed_hbm.1) | copy-start | bytes 76

commit v4 on v3

--- a/solution.py
+++ b/solution.py
@@ -234,9 +234,12 @@
         high.append(jnp.concatenate([down_h, up_h], axis=1))
         rest.append(jnp.concatenate([down_r, up_r], axis=1))
     weights = basis_ref[level % 2]
-    both = jnp.dot(jnp.concatenate(high, axis=0), weights, preferred_element_type=F32)
-    both = both + jnp.dot(jnp.concatenate(rest, axis=0), weights, preferred_element_type=F32)
-    result = both[:, :128] + both[:, 128:]
+    twice = jnp.concatenate([weights, weights], axis=0)
+    result = []
+    for h, r in zip(high, rest):
+        both = jnp.dot(jnp.concatenate([h, r], axis=1), twice, preferred_element_type=F32)
+        result.append(both[:, :128] + both[:, 128:])
+    result = jnp.concatenate(result, axis=0)
     after = [p for p, _ in pairs] + [q for _, q in pairs]
     return {at: result[8 * n : 8 * n + 8] for n, at in enumerate(after)}
 

time: 32.4 us -> 31.2 us (0.963)
  Pallas kernels: 29.8 us -> 28.9 us
    pallas_call x1, Pallas kernels: 29.8 us -> 28.9 us  [on_device(): pl.pallas_call(kernel, out_shape=jax.ShapeDtypeStruct((16, 16, 8, 128), F...]
where the time goes in v4:
time: 31.2 us; the launch traced here: 31 us
  Pallas kernels  28.9 us (93%)
  other arithmetic  1.14 us (4%)
  local copies, waits for them, and re-layouts  0.98 us (3%)
    pallas_call x1, Pallas kernels, on_device(): pl.pallas_call(kernel, out_shape=jax.ShapeDtypeStruct((16, 16, 8, 128), F...  28.9 us
    reshape x1, other arithmetic, on_device(): source_weights.astype(F32).reshape(2, 1024, 128)  1.14 us
    unnamed x5, local copies, waits for them, and re-layouts  0.98 us

profile of v4, /device:TPU:1, one launch (start us, length us, event | category | flops | bytes accessed | tf_op | source)
XLA Modules:
  0.0 31.0 jit_solution(17241424619304235651)
XLA Ops:
  0.0 0.0 copy-start
  0.0 0.0 copy-start.1
  0.0 1.1 %bitcast_convert_fusion.wide = f32[2,1024,128]{2,1,0:T(8,128)S(1)} fusion(bf16[2,1,1024,128]{3,2,1,0:T(8,128)(2,1)} %param.3), kind=kLoop, calls=%fused_computation | loop fusion | flops 262144 | bytes 1572864 | tf_op jit(solution)/shard_map/reshape | solution.py:388
  1.1 0.0 copy-done
  1.2 0.0 copy-done.1
  1.2 28.9 %shard_map.37 = f32[16,16,8,128]{3,2,1,0:T(8,128)S(1)} custom-call(f32[2,3]{1,0:T(2,128)S(1)} %copy-done.1, f32[4,32]{1,0:T(4,128)S(1)} %bitcast.6, f32[2,1024,128]{2,1,0:T(8,128)S(1)} %bitcast_convert_fusion.wide), custom_call_target="tpu_custom_call" | custom-call | tf_op jit(solution)/shard_map/pallas_call | solution.py:369
  30.1 1.0 %copy.6 = f32[16,16,8,128]{3,2,1,0:T(8,128)} copy(f32[16,16,8,128]{3,2,1,0:T(8,128)S(1)} %shard_map.37) | data formatting | bytes 2097152
Async XLA Ops:
  0.0 1.1 %copy-start = (f32[32,4]{0,1:T(4,128)S(1)}, f32[32,4]{0,1:T(4,128)}, u32[]{:S(2)}) copy-start(f32[32,4]{0,1:T(4,128)} %param.5) | copy-start | bytes 1540
  0.0 1.2 %copy-start.1 = (f32[2,3]{1,0:T(2,128)S(1)}, f32[2,3]{1,0:T(2,128)}, u32[]{:S(2)}) copy-start(f32[2,3]{1,0:T(2,128)} %speed_hbm.1) | copy-start | bytes 76

commit v5 on v4

--- a/solution.py
+++ b/solution.py
@@ -252,7 +252,7 @@
     order = []
     for start in (0, 2, 1, 3):
         parts = (start, start + 8, start + 4, start + 12)
-        quarter = [((3 * i + 5 * u) % 8, b) for i in range(8) for u, b in enumerate(parts)]
+        quarter = [((i + 2 * u) % 8, b) for i in range(8) for u, b in enumerate(parts)]
         order += sorted(quarter, key=lambda to: -hops(*to))
     return [to for to in order if to != (0, 0)]
 
@@ -297,7 +297,7 @@
     pl.semaphore_wait(barrier, n - 1)
 
     def columns(owner):
-        return wide.at[:, pl.ds(pl.multiple_of(owner * 8, 8), 8), :]
+        return wide.at[owner]
 
     pltpu.make_async_copy(columns(me), data.at[tgt, src], recv_sem.at[0]).start()
 
@@ -385,7 +385,7 @@
         compiler_params=pltpu.CompilerParams(
             collective_id=0, has_side_effects=True, vmem_limit_bytes=VMEM_BYTES
         ),
-    )(wave_speed, offsets.T, source_weights.astype(F32).reshape(2, 1024, 128))
+    )(wave_speed, offsets.T, source_weights.astype(F32).reshape(2, 128, 8, 128).transpose(1, 0, 2, 3))
 
 
 def solution(mesh):

time: 31.2 us -> 30.9 us (level)
    reshape x1 -> x0, other arithmetic: 1.14 us -> none  [on_device(): source_weights.astype(F32).reshape(2, 1024, 128)]
    transpose x0 -> x1, other arithmetic: none -> 1.14 us  [on_device(): source_weights.astype(F32).reshape(2, 128, 8, 128).transpose(1, 0, 2, 3)]
where the time goes in v5:
time: 30.9 us; the launch traced here: 30.8 us
  Pallas kernels  28.6 us (93%)
  other arithmetic  1.14 us (4%)
  local copies, waits for them, and re-layouts  0.98 us (3%)
    pallas_call x1, Pallas kernels, on_device(): pl.pallas_call(kernel, out_shape=jax.ShapeDtypeStruct((16, 16, 8, 128), F...  28.6 us
    transpose x1, other arithmetic, on_device(): source_weights.astype(F32).reshape(2, 128, 8, 128).transpose(1, 0, 2, 3)  1.14 us
    unnamed x5, local copies, waits for them, and re-layouts  0.98 us

profile of v5, /device:TPU:1, one launch (start us, length us, event | category | flops | bytes accessed | tf_op | source)
XLA Modules:
  0.0 30.8 jit_solution(13467061377449236646)
XLA Ops:
  0.0 0.0 copy-start
  0.0 0.0 copy-start.1
  0.0 1.1 %copy_bitcast_fusion.wide = f32[128,2,8,128]{3,2,1,0:T(8,128)S(1)} fusion(bf16[2,1,1024,128]{3,2,1,0:T(8,128)(2,1)} %param.3), kind=kLoop, calls=%fused_computation | loop fusion | flops 262144 | bytes 1572864 | tf_op jit(solution)/shard_map/transpose | solution.py:388
  1.1 0.0 copy-done
  1.2 0.0 copy-done.1
  1.2 28.6 %shard_map.37 = f32[16,16,8,128]{3,2,1,0:T(8,128)S(1)} custom-call(f32[2,3]{1,0:T(2,128)S(1)} %copy-done.1, f32[4,32]{1,0:T(4,128)S(1)} %bitcast.9, f32[128,2,8,128]{3,2,1,0:T(8,128)S(1)} %copy_bitcast_fusion.wide), custom_call_target="tpu_custom_call" | custom-call | tf_op jit(solution)/shard_map/pallas_call | solution.py:369
  29.8 1.0 %copy.8 = f32[16,16,8,128]{3,2,1,0:T(8,128)} copy(f32[16,16,8,128]{3,2,1,0:T(8,128)S(1)} %shard_map.37) | data formatting | bytes 2097152
Async XLA Ops:
  0.0 1.2 %copy-start = (f32[32,4]{0,1:T(4,128)S(1)}, f32[32,4]{0,1:T(4,128)}, u32[]{:S(2)}) copy-start(f32[32,4]{0,1:T(4,128)} %param.5) | copy-start | bytes 1540
  0.0 1.2 %copy-start.1 = (f32[2,3]{1,0:T(2,128)S(1)}, f32[2,3]{1,0:T(2,128)}, u32[]{:S(2)}) copy-start(f32[2,3]{1,0:T(2,128)} %speed_hbm.1) | copy-start | bytes 76
